TPU v7x, 32 devices: a whole 2x2x4 slice. The times are simulated.
32 devices in a mesh: sec: 8 (over z, y), blk: 4 (over x, core).
Axes of the slice: x: 2, y: 2, z: 4, core: 2. Of those that a mesh axis runs over, the one named last changes fastest.
Arguments:
- wave: bfloat16 [8, 4, 256, 256], P('sec', 'blk'), may hold values from -6 to 6
- left_block_environment: bfloat16 [8, 4, 16, 256, 256], P('sec', 'blk'), may hold values from -0.375 to 0.375
- right_block_environment: bfloat16 [8, 4, 16, 256, 256], P('sec', 'blk'), may hold values from -0.09375 to 0.09375
- source_block: int32 [8, 4, 16], P('sec', 'blk'), may hold values from 0 to 3
- sector_size: int32 [8, 4], P('sec', 'blk'), may hold values from 1 to 256, 640 in all within a row
Outputs:
- first_product: bfloat16 [8, 4, 256, 256], P('sec', 'blk')
- second_product: bfloat16 [8, 4, 256, 256], P('sec', 'blk')
All inputs are finite; a program needn't handle non-finite values. No bound on the sum of `sector_size` on one device may be relied on, other than what follows from the above.
Results may differ from a plain program's by a relative error of at most 0.015.
Values may be sent and summed in bfloat16 or wider, within the bound.
A program may use at most 64 MiB of HBM per device.

v0:
```python
import math

import jax
import jax.numpy as jnp
from jax import lax
from jax.sharding import PartitionSpec as P


def shifted(value, axis, steps):
    count = lax.axis_size(axis)
    initial, last = (max(0, -steps), min(count, count - steps))
    return lax.ppermute(value, axis, [(source, source + steps) for source in range(initial, last)])


def live_mask(sizes, width):
    rows = jnp.arange(width, dtype=jnp.int32)
    first = rows[None, :, None] < sizes[:, None, None]
    second_apply = rows[None, None, :] < sizes[:, None, None]
    return (first & second_apply).astype(jnp.bfloat16)


def apply_blocks(left, pool, picks, right):
    chosen = jnp.take(pool, picks, axis=0)
    inner = jnp.einsum("ktab,ktbc->ktac", left, chosen, preferred_element_type=jnp.float32).astype(
        jnp.bfloat16
    )
    return jnp.einsum("ktab,ktbc->kac", inner, right, preferred_element_type=jnp.float32)


def shards(wave, left_block_environment, right_block_environment, source_block, sector_size):
    left = left_block_environment[0]
    right = right_block_environment[0]
    picks = source_block[0]
    sizes = sector_size[0]
    blocks = wave.shape[1]
    width = wave.shape[2]
    mask = live_mask(sizes, width)
    mask_f = mask.astype(jnp.float32)
    live = wave[0] * mask
    pool = lax.all_gather(live, "blk", axis=0, tiled=True)
    first = (apply_blocks(left, pool, picks, right) * mask_f).astype(jnp.bfloat16)
    first_f = first.astype(jnp.float32)
    squares = jnp.sum(first_f * first_f)
    count = jnp.sum((sizes * sizes).astype(jnp.float32))
    totals = lax.psum((squares, count), "blk")
    scale = lax.rsqrt(totals[0] / totals[1] + 1e-06)
    trial_vector = (first_f * scale).astype(jnp.bfloat16)
    second_pool_result = lax.all_gather(trial_vector, "blk", axis=0, tiled=True)
    left_vector = jnp.einsum(
        "ktab,kbc->ktac", left, trial_vector, preferred_element_type=jnp.float32
    ).astype(jnp.bfloat16)
    partial_border_sum = jnp.einsum(
        "glj,gdls->djs", trial_vector, left_vector, preferred_element_type=jnp.float32
    )
    factor = 1.0 / (width * math.sqrt(blocks * lax.axis_size("blk")))
    share = lax.psum_scatter(
        partial_border_sum.astype(jnp.bfloat16), "blk", scatter_dimension=1, tiled=True
    ).astype(jnp.float32)
    edge = (share * factor).astype(jnp.bfloat16)
    moved = shifted(edge, "sec", 1)
    incoming = lax.all_gather(moved, "blk", axis=1, tiled=True)
    left_two = left + incoming[None]
    second_apply = (apply_blocks(left_two, second_pool_result, picks, right) * mask_f).astype(
        jnp.bfloat16
    )
    return (first[None], second_apply[None])


def solution(mesh):
    return jax.shard_map(
        shards,
        mesh=mesh,
        in_specs=(
            P("sec", "blk", None, None),
            P("sec", "blk", None, None, None),
            P("sec", "blk", None, None, None),
            P("sec", "blk", None),
            P("sec", "blk"),
        ),
        out_specs=(P("sec", "blk", None, None), P("sec", "blk", None, None)),
        check_vma=False,
    )
```

profile of v0, /device:TPU:11, one launch (start us, length us, event | category | flops | bytes accessed | tf_op | source)
XLA Modules:
  0.0 122.7 jit_solution(939255838413143524)
XLA Ops:
  7.2 0.0 copy-start
  7.2 0.0 reduce-scatter.2.cloned.1.call-start
  7.2 0.8 fusion.100
  8.0 0.7 and_bitcast_fusion
  9.3 1.0 and_select_fusion
  10.4 7.3 %all_gather.9 = bf16[4,256,256]{2,1,0:T(8,128)(2,1)S(1)} all-gather(bf16[1,256,256]{2,1,0:T(8,128)(2,1)S(1)} %and_select_fusion), channel_id=1, replica_groups=mesh['sec'=8,'blk'=4] {'blk'}, dimensions={0}, use_global_device_ids=true | all-gather | bytes 655360 | tf_op jit(solution)/shard_map/all_gather | solution.py:40
  17.7 2.0 %gather_fusion = bf16[16,256,256]{2,1,0:T(8,128)(2,1)} fusion(bf16[4,256,256]{2,1,0:T(8,128)(2,1)S(1)} %all_gather.9, s32[1024]{0:T(1024)S(1)} %pad_clamp_fusion), kind=kCustom, calls=%fused_computation.clone | custom fusion | bytes 4194368 | tf_op jit(solution)/shard_map/jit(_take)/gather | solution.py:23
  19.7 0.0 copy-done
  19.7 4.3 %fusion.92 = (f32[]{:T(128)}, bf16[256,256]{1,0:T(8,128)(2,1)S(1)}) fusion(pred[256]{0:T(512)(128)(4,1)S(1)} %iota_compare_fusion, bf16[1,1,16,256,256]{4,3,2,1,0:T(8,128)(2,1)S(1)} %copy-done, bf16[16,256,256]{2,1,0:T(8,128)(2,1)} %gather_fusion, pred[16]{0:T(512)(128)(4,1)S(1)} %and_bitcast_fusion, bf16[1,1,16,256,256]{4,3,2,1,0:T(8,128)(2,1)} %param.8), kind=kOutput, calls=%fused_computation.38 | convolution fusion | flops 1076363264 | bytes 6422804 | tf_op jit(solution)/shard_map/ktab,ktbc->kac/dot_general | solution.py:27
  23.9 0.0 copy-start.2
  23.9 6.3 %all-reduce = (f32[]{:T(128)}, f32[]{:T(128)}) all-reduce(f32[]{:T(128)} %get-tuple-element.5, f32[]{:T(128)} %bitcast.12), channel_id=1, replica_groups=mesh['sec'=8,'blk'=4] {'blk'}, use_global_device_ids=true, to_apply=%region_1.3 | all-reduce | flops 2 | bytes 16 | tf_op jit(solution)/shard_map/psum | solution.py:45
  31.7 2.4 %fusion.8 = bf16[256,16,256]{2,0,1:T(8,128)(2,1)S(1)} fusion(bf16[1,1,16,256,256]{4,3,2,1,0:T(8,128)(2,1)} %param.8, bf16[256,256]{1,0:T(8,128)(2,1)S(1)} %fusion.93), kind=kOutput, calls=%fused_computation.13 | convolution fusion | flops 536870912 | bytes 4325376 | tf_op jit(solution)/shard_map/ktab,kbc->ktac/dot_general | solution.py:49
  34.0 0.0 copy-done.2
  34.0 1.2 copy.16
  35.2 2.4 %convert_bitcast_fusion = bf16[16,256,256]{2,1,0:T(8,128)(2,1)} fusion(bf16[16,256,256]{1,0,2:T(8,128)(2,1)S(1)} %bitcast.173, bf16[256,256]{1,0:T(8,128)(2,1)S(1)} %fusion.93), kind=kOutput, calls=%fused_computation.22 | convolution fusion | flops 537919488 | bytes 4325376 | tf_op jit(solution)/shard_map/glj,gdls->djs/dot_general | solution.py:52
  37.6 0.0 reduce-scatter.2.cloned.1.call-update
  37.6 0.0 all-gather.3.cloned.1.call-start
  37.7 32.6 %reduce-scatter.2.cloned.1.call-done = bf16[16,64,256]{2,1,0:T(8,128)(2,1)} async-done(((bf16[16,256,256]{2,1,0:T(8,128)(2,1)}), bf16[16,64,256]{2,1,0:T(8,128)(2,1)}) %reduce-scatter.2.cloned.1.call-update) | async-done | bytes 524304 | tf_op jit(solution)/shard_map/reduce_scatter | solution.py:56
  70.2 1.1 multiply_convert_fusion
  71.4 3.1 %collective-permute-start = (bf16[16,64,256]{2,1,0:T(8,128)(2,1)S(1)}, bf16[16,64,256]{2,1,0:T(8,128)(2,1)S(1)}, u32[]{:S(2)}, u32[]{:S(2)}) collective-permute-start(bf16[16,64,256]{2,1,0:T(8,128)(2,1)S(1)} %multiply_convert_fusion), channel_id=1, source_target_pairs={{0,4},{4,8},{8,12},{12,16},{16,20},{20,24},{24,28},{1,5},{5,9},{9,... | collective-permute-start | bytes 1572872 | tf_op jit(solution)/shard_map/ppermute | solution.py:12
  74.5 12.5 %collective-permute-done = bf16[16,64,256]{2,1,0:T(8,128)(2,1)S(1)} collective-permute-done((bf16[16,64,256]{2,1,0:T(8,128)(2,1)S(1)}, bf16[16,64,256]{2,1,0:T(8,128)(2,1)S(1)}, u32[]{:S(2)}, u32[]{:S(2)}) %collective-permute-start) | collective-permute-done | bytes 524320 | tf_op jit(solution)/shard_map/ppermute | solution.py:12
  87.0 0.0 copy-start.1
  87.0 0.8 copy-done.1
  87.8 0.0 all-gather.3.cloned.1.call-update
  87.8 8.5 %all-gather = bf16[1024,256]{1,0:T(8,128)(2,1)S(1)} all-gather(bf16[256,256]{1,0:T(8,128)(2,1)S(1)} %fusion.93), channel_id=2, replica_groups=mesh['sec'=8,'blk'=4] {'blk'}, dimensions={0}, use_global_device_ids=true | all-gather | bytes 655360 | tf_op jit(solution)/shard_map/all_gather | solution.py:48
  96.4 2.0 %gather_fusion.1 = bf16[16,256,256]{2,1,0:T(8,128)(2,1)} fusion(bf16[4,256,256]{2,1,0:T(8,128)(2,1)S(1)} %bitcast.172, s32[1024]{0:T(1024)S(1)} %pad_clamp_fusion), kind=kCustom, calls=%fused_computation.1.clone | custom fusion | bytes 4194368 | tf_op jit(solution)/shard_map/jit(_take)/gather | solution.py:23
  98.3 12.6 %all-gather.3.cloned.1.call-done = bf16[16,256,256]{2,1,0:T(8,128)(2,1)} async-done(((bf16[16,64,256]{2,1,0:T(8,128)(2,1)}), bf16[16,256,256]{2,1,0:T(8,128)(2,1)}) %all-gather.3.cloned.1.call-update) | async-done | bytes 2097168 | tf_op jit(solution)/shard_map/all_gather | solution.py:61
  110.9 5.0 %fusion.81 = bf16[1,1,256,256]{3,2,1,0:T(8,128)(2,1)} fusion(bf16[1,1,16,256,256]{4,3,2,1,0:T(8,128)(2,1)S(1)} %copy-done, bf16[16,256,256]{2,1,0:T(8,128)(2,1)} %gather_fusion.1, pred[16]{0:T(512)(128)(4,1)S(1)} %and_bitcast_fusion, bf16[16,256,256]{2,1,0:T(8,128)(2,1)} %all-gather.3.cloned.1.call-done, bf16[1,1,16,256,256]{4,3,2,1,0:T(8,128)(2,1)} %param.8, ...), kind=kOutput, calls=%fused_computation.32 | convolution fusion | flops 1077215232 | bytes 8519952 | tf_op jit(solution)/shard_map/ktab,ktbc->kac/dot_general | solution.py:27
  (3 shorter events, 0.0 us)
Async XLA Ops:
  7.2 12.5 %copy-start = (bf16[1,1,16,256,256]{4,3,2,1,0:T(8,128)(2,1)S(1)}, bf16[1,1,16,256,256]{4,3,2,1,0:T(8,128)(2,1)}, u32[]{:S(2)}) copy-start(bf16[1,1,16,256,256]{4,3,2,1,0:T(8,128)(2,1)} %param.9) | copy-start | bytes 6291460
  7.2 63.1 %reduce-scatter.2.cloned.1.call-start = ((), (), s32[]{:S(2)}) async-start(), calls=%async_computation.1 | async-start | bytes 2621440 | tf_op jit(solution)/shard_map/reduce_scatter | solution.py:56
  23.9 10.1 %copy-start.2 = (bf16[256,256]{1,0:T(8,128)(2,1)}, bf16[256,256]{1,0:T(8,128)(2,1)S(1)}, u32[]{:S(2)}) copy-start(bf16[256,256]{1,0:T(8,128)(2,1)S(1)} %get-tuple-element.6) | copy-start | bytes 393220
  37.6 73.3 %all-gather.3.cloned.1.call-start = ((), (), s32[]{:S(2)}) async-start(), calls=%async_computation.2 | async-start | bytes 2621440 | tf_op jit(solution)/shard_map/all_gather | solution.py:61
  71.4 15.6 %collective-permute-start = (bf16[16,64,256]{2,1,0:T(8,128)(2,1)S(1)}, bf16[16,64,256]{2,1,0:T(8,128)(2,1)S(1)}, u32[]{:S(2)}, u32[]{:S(2)}) collective-permute-start(bf16[16,64,256]{2,1,0:T(8,128)(2,1)S(1)} %multiply_convert_fusion), channel_id=1, source_target_pairs={{0,4},{4,8},{8,12},{12,16},{16,20},{20,24},{24,28},{1,5},{5,9},{9,... | collective-permute-start | bytes 1572872 | tf_op jit(solution)/shard_map/ppermute | solution.py:12
  87.0 0.8 copy-start.1
Sparse Core Ops, SparseCore 0:
  37.8 32.4 reduce-scatter.1
  87.9 22.9 all-gather.2
where the time goes:
time: 125 us; the launch traced here: 123 us
  waiting for transfers between devices  57.7 us (46%)
  blocking collectives  22.2 us (18%)
  between operations  16.1 us (13%)
  matrix products  14 us (11%)
  local copies, waits for them, and re-layouts  6.01 us (5%)
  other arithmetic  3.64 us (3%)
  starting transfers between devices  3.2 us (3%)
    reduce_scatter x1, waiting for transfers between devices, shards(): lax.psum_scatter(partial_border_sum.astype(jnp.bfloat16), 'blk', scatter_...  32.6 us
    all_gather x1, waiting for transfers between devices, shards(): incoming = lax.all_gather(moved, 'blk', axis=1, tiled=True)  12.6 us
    ppermute x1, waiting for transfers between devices, shifted(): lax.ppermute(value, axis, [(source, source + steps) for source in range(i...  12.5 us
    dot_general x2, matrix products, apply_blocks(): jnp.einsum('ktab,ktbc->kac', inner, right, preferred_element_type=jnp.flo...  9.21 us
    all_gather x1, blocking collectives, shards(): second_pool_result = lax.all_gather(trial_vector, 'blk', axis=0, tiled=True)  8.55 us
    all_gather x1, blocking collectives, shards(): pool = lax.all_gather(live, 'blk', axis=0, tiled=True)  7.29 us
    psum x1, blocking collectives, shards(): totals = lax.psum((squares, count), 'blk')  6.33 us
    gather x2, local copies, waits for them, and re-layouts, apply_blocks(): chosen = jnp.take(pool, picks, axis=0)  4 us
  transfers between devices with their start and end apart: 3, of which 3 were waited for; matrix products, arithmetic and copies ran while one was open for 2% of the time, Pallas kernels for 0%

commit v1 on v0

v1 whole, which is shorter than its diff:
```python
import functools
import math

import jax
import jax.numpy as jnp
from jax import lax
from jax.experimental import pallas as pl
from jax.experimental.pallas import tpu as pltpu
from jax.sharding import PartitionSpec as P

MESH = pl.DeviceIdType.MESH
F32 = jnp.float32
BF16 = jnp.bfloat16


def dot(a, b):
    return jnp.dot(a, b, preferred_element_type=F32)


def copies_between(nb, per):
    nx = nb // 2
    return 2 * (2 * nx - 1) + (nb - 1) + nx * per + (nx - 1) * per + per + per * (2 * nx - 1)


def kernel(
    nsec, nb, picks, sizes, wave_h, left_h, right_h, out1_h, out2_h,
    wave_v, left, right, pool, fpool, inner, psend, precv, mine, rsend, rrecv, edge, inc, meta, acc,
    stage, lsem, ssem, rsem,
):
    width = wave_h.shape[-1]
    channels = left_h.shape[0]
    nx = nb // 2
    per = channels // nb
    sec = lax.axis_index("sec")
    me = lax.axis_index("blk")
    chip = me // 2
    core = me % 2
    sib = chip * 2 + 1 - core

    load_wave = pltpu.make_async_copy(wave_h, wave_v, lsem.at[0])
    load_left = pltpu.make_async_copy(left_h, left, lsem.at[1])
    load_right = pltpu.make_async_copy(right_h, right, lsem.at[2])
    load_wave.start()
    load_left.start()
    load_right.start()

    barrier = pltpu.get_barrier_semaphore()
    for o in range(1, nb):
        pl.semaphore_signal(barrier, inc=1, device_id={"blk": (me + o) % nb}, device_id_type=MESH)

    @pl.when(sec > 0)
    def _():
        pl.semaphore_signal(barrier, inc=1, device_id={"sec": sec - 1}, device_id_type=MESH)

    @pl.when(sec < nsec - 1)
    def _():
        pl.semaphore_signal(barrier, inc=1, device_id={"sec": sec + 1}, device_id_type=MESH)

    at = {}
    sent = []

    def remote(key, src, dst, **device):
        k = at.setdefault(key, len(at))
        return pltpu.make_async_remote_copy(
            src_ref=src, dst_ref=dst, send_sem=ssem.at[k], recv_sem=rsem.at[k],
            device_id=device, device_id_type=MESH,
        )

    def send(key, src, dst, **device):
        copy = remote(key, src, dst, **device)
        copy.start()
        sent.append(copy)

    def arrived(key, ref):
        remote(key, ref, ref, blk=sib).wait_recv()

    def same_core(o):
        return ((chip + o) % nx) * 2 + core

    def share(name, ref):
        for o in range(1, nx):
            send((name, "x", o), ref.at[me], ref.at[me], blk=same_core(o))
        send((name, "c", 0), ref.at[me], ref.at[me], blk=sib)

    def pass_on(name, ref):
        for o in range(1, nx):
            block = ref.at[same_core(nx - o)]
            arrived((name, "x", o), block)
            send((name, "c", o), block, block, blk=sib)

    def take(name, ref):
        for o in range(nx):
            arrived((name, "c", o), ref.at[((chip + nx - o) % nx) * 2 + 1 - core])

    size = sizes[0]
    live_at = (lax.broadcasted_iota(jnp.int32, (width, width), 0) < size) & (
        lax.broadcasted_iota(jnp.int32, (width, width), 1) < size
    )
    load_wave.wait()
    pool[me] = jnp.where(live_at, wave_v[...].astype(F32), 0.0).astype(BF16)
    pl.semaphore_wait(
        barrier, nb - 1 + (sec > 0).astype(jnp.int32) + (sec < nsec - 1).astype(jnp.int32)
    )
    share("live", pool)
    load_left.wait()
    load_right.wait()
    pass_on("live", pool)
    take("live", pool)

    for t in range(channels):
        inner[:, t * width:(t + 1) * width] = dot(left[t], pool[picks[t]]).astype(BF16)
    total = dot(inner[...], right[...].reshape(channels * width, width))
    first = jnp.where(live_at, total, 0.0).astype(BF16)
    fpool[me] = first
    share("first", fpool)
    store_first = pltpu.make_async_copy(fpool.at[me], out1_h, lsem.at[3])
    store_first.start()

    first_f = fpool[me].astype(F32)
    first_t = jnp.transpose(first_f).astype(BF16)

    rounds = [(o, j) for o in list(range(1, nx)) + [0] for j in range(per)]

    def combine(r):
        o, j = rounds[r]
        arrived(("part", r), precv.at[r])
        both = mine[r].astype(F32) + precv[r].astype(F32)
        if o == 0:
            acc_at = j
            edge[acc_at] = both.astype(BF16)
        else:
            slot = (o - 1) * per + j
            rsend[slot] = both.astype(BF16)
            send(("rs", o, j), rsend.at[slot], rrecv.at[slot], blk=same_core(o))

    for r, (o, j) in enumerate(rounds):
        q = (chip + o) % nx
        theirs = (q * 2 + 1 - core) * per + j
        own = (q * 2 + core) * per + j
        lv = dot(left[theirs], fpool[me]).astype(BF16)
        psend[r] = dot(first_t, lv).astype(BF16)
        send(("part", r), psend.at[r], precv.at[r], blk=sib)
        lv = dot(left[own], fpool[me]).astype(BF16)
        mine[r] = dot(first_t, lv).astype(BF16)
        if r == 0:
            squares = jnp.sum((first_f * first_f).reshape(width // 8, 8, width), axis=0)
            fold = squares[:, :128]
            for c in range(128, width, 128):
                fold = fold + squares[:, c:c + 128]
            meta[me, :8] = fold
            meta[me, 8:] = jnp.full((8, 128), (size * size).astype(F32), F32)
            for p in range(1, nb):
                send(("meta", p), meta.at[me], meta.at[me], blk=(me + p) % nb)
        if r >= 1:
            combine(r - 1)
    combine(len(rounds) - 1)

    pass_on("first", fpool)
    for p in range(1, nb):
        arrived(("meta", p), meta.at[(me + nb - p) % nb])
    totals = jnp.sum(meta[...], axis=0)
    square_sum = jnp.sum(totals[:8], keepdims=True)
    count = jnp.sum(totals[8:], keepdims=True) * (1.0 / 1024)
    scale = lax.rsqrt(square_sum / count + 1e-06)
    factor = scale * scale * (1.0 / (width * math.sqrt(nb)))
    store_first.wait()
    take("first", fpool)

    later = []

    def up(j):
        result = edge[j].astype(F32)
        for o in range(1, nx):
            slot = (o - 1) * per + j
            arrived(("rs", o, j), rrecv.at[slot])
            result = result + rrecv[slot].astype(F32)
        edge[j] = (result * factor).astype(BF16)
        copy = remote(("up", j), edge.at[j], inc.at[me * per + j], sec=sec + 1)
        later.append(copy)

        @pl.when(sec < nsec - 1)
        def _():
            copy.start()

    inner_sends = []

    def spread(j):
        t = me * per + j
        block = inc.at[t]
        outs = [remote(("inc", j, "x", o), block, block, blk=same_core(o)) for o in range(1, nx)]
        outs.append(remote(("inc", j, "c", 0), block, block, blk=sib))
        inner_sends.extend(outs)

        @pl.when(sec > 0)
        def _():
            arrived(("up", j), block)
            for copy in outs:
                copy.start()

    def hand_on(j):
        pairs = []
        for o in range(1, nx):
            block = inc.at[same_core(nx - o) * per + j]
            pairs.append((o, block, remote(("inc", j, "c", o), block, block, blk=sib)))
        inner_sends.extend(copy for _, _, copy in pairs)

        @pl.when(sec > 0)
        def _():
            for o, block, copy in pairs:
                arrived(("inc", j, "x", o), block)
                copy.start()

    def second(j):
        @pl.when(sec > 0)
        def _():
            for o in range(nx):
                arrived(("inc", j, "c", o), inc.at[(((chip + nx - o) % nx) * 2 + 1 - core) * per + j])

        result = acc[...] if j else None
        for d in range(nb):
            t = d * per + j
            left_two = (left[t].astype(F32) + inc[t].astype(F32)).astype(BF16)
            step = dot(dot(left_two, fpool[picks[t]]).astype(BF16), right[t])
            result = step if result is None else result + step
        acc[...] = result

    @pl.when(sec == 0)
    def _():
        inc[...] = jnp.zeros_like(inc)

    for tick in range(per + 4):
        if tick < per:
            up(tick)
        if 1 <= tick < per + 1:
            spread(tick - 1)
        if 2 <= tick < per + 2:
            hand_on(tick - 2)
        if 3 <= tick < per + 3:
            second(tick - 3)

    stage[...] = jnp.where(live_at, acc[...] * scale, 0.0).astype(BF16)
    store_second = pltpu.make_async_copy(stage, out2_h, lsem.at[4])
    store_second.start()

    for copy in sent:
        copy.wait_send()

    @pl.when(sec < nsec - 1)
    def _():
        for copy in later:
            copy.wait_send()

    @pl.when(sec > 0)
    def _():
        for copy in inner_sends:
            copy.wait_send()

    store_second.wait()


def shards(nsec, nb, wave, left, right, picks, sizes):
    width = wave.shape[-1]
    channels = left.shape[2]
    nx = nb // 2
    per = channels // nb
    block = (width, width)
    copies = copies_between(nb, per)
    vmem = lambda *lead: pltpu.VMEM((*lead, *block), BF16)
    anywhere = pl.BlockSpec(memory_space=pl.ANY)
    smem = pl.BlockSpec(memory_space=pltpu.SMEM)
    out = jax.ShapeDtypeStruct(block, BF16)
    first, second = pl.pallas_call(
        functools.partial(kernel, nsec, nb),
        out_shape=(out, out),
        in_specs=[smem, smem, anywhere, anywhere, anywhere],
        out_specs=(anywhere, anywhere),
        scratch_shapes=[
            vmem(),
            vmem(channels),
            vmem(channels),
            vmem(nb),
            vmem(nb),
            pltpu.VMEM((width, channels * width), BF16),
            vmem(nx * per),
            vmem(nx * per),
            vmem(nx * per),
            vmem((nx - 1) * per),
            vmem((nx - 1) * per),
            vmem(per),
            vmem(channels),
            pltpu.VMEM((nb, 16, 128), F32),
            pltpu.VMEM(block, F32),
            vmem(),
            pltpu.SemaphoreType.DMA((5,)),
            pltpu.SemaphoreType.DMA((copies,)),
            pltpu.SemaphoreType.DMA((copies,)),
        ],
        compiler_params=pltpu.CompilerParams(
            collective_id=0, has_side_effects=True, vmem_limit_bytes=48 * 2**20
        ),
        cost_estimate=pl.CostEstimate(
            flops=12 * channels * width**3, bytes_accessed=4 * channels * width**2, transcendentals=0
        ),
    )(
        picks.reshape(channels),
        sizes.reshape(1),
        wave.reshape(block),
        left.reshape(channels, *block),
        right.reshape(channels, *block),
    )
    return first[None, None], second[None, None]


def solution(mesh):
    return jax.shard_map(
        functools.partial(shards, mesh.shape["sec"], mesh.shape["blk"]),
        mesh=mesh,
        in_specs=(
            P("sec", "blk", None, None),
            P("sec", "blk", None, None, None),
            P("sec", "blk", None, None, None),
            P("sec", "blk", None),
            P("sec", "blk"),
        ),
        out_specs=(P("sec", "blk", None, None), P("sec", "blk", None, None)),
        check_vma=False,
    )
```

time: 125 us -> 49.5 us (0.40); the launches traced: 123 us -> 49.3 us
  waiting for transfers between devices: 57.7 us -> 0 us
  Pallas kernels: 0 us -> 41.9 us
  blocking collectives: 22.2 us -> 0 us
  between operations: 16.1 us -> 1.3 us
  matrix products: 14 us -> 0 us
  other arithmetic: 3.64 us -> 0 us
  starting transfers between devices: 3.2 us -> 0 us
    pallas_call x0 -> x1, Pallas kernels: none -> 41.9 us  [shards(): pl.pallas_call(functools.partial(kernel, nsec, nb), out_shape=(out, out),...]
    reduce_scatter x1 -> x0, waiting for transfers between devices: 32.6 us -> none  [shards(): lax.psum_scatter(partial_border_sum.astype(jnp.bfloat16), 'blk', scatter_...]
    all_gather x2 -> x0, blocking collectives: 15.8 us -> none  [the longest x1 8.55 us: shards(): second_pool_result = lax.all_gather(trial_vector, 'blk', axis=0, tiled=True)]
    dot_general x4 -> x0, matrix products: 14 us -> none  [the longest x2 9.21 us: apply_blocks(): jnp.einsum('ktab,ktbc->kac', inner, right, preferred_element_type=jnp.flo...]
    all_gather x1 -> x0, waiting for transfers between devices: 12.6 us -> none  [shards(): incoming = lax.all_gather(moved, 'blk', axis=1, tiled=True)]
    ppermute x1 -> x0, waiting for transfers between devices: 12.5 us -> none  [shifted(): lax.ppermute(value, axis, [(source, source + steps) for source in range(i...]
    psum x1 -> x0, blocking collectives: 6.33 us -> none  [shards(): totals = lax.psum((squares, count), 'blk')]
    unnamed x6 -> x10, local copies, waits for them, and re-layouts: 0.82 us -> 6.05 us
  transfers between devices with their start and end apart: 3 -> 0, of which waited for: 3 -> 0; matrix products, arithmetic and copies ran while one was open for 2% -> 0% of each run, Pallas kernels for 0% -> 0%
where the time goes in v1:
time: 49.5 us; the launch traced here: 49.3 us
  Pallas kernels  41.9 us (85%)
  local copies, waits for them, and re-layouts  6.05 us (12%)
  between operations  1.3 us (3%)
    pallas_call x1, Pallas kernels, shards(): pl.pallas_call(functools.partial(kernel, nsec, nb), out_shape=(out, out),...  41.9 us
    unnamed x10, local copies, waits for them, and re-layouts  6.05 us

profile of v1, /device:TPU:11, one launch (start us, length us, event | category | flops | bytes accessed | tf_op | source)
XLA Modules:
  0.0 49.3 jit_solution(9675214257276720707)
XLA Ops:
  1.3 0.0 copy-start
  1.3 1.6 %copy-done = bf16[1,1,16,256,256]{4,3,2,1,0:T(8,128)(2,1)S(1)} copy-done((bf16[1,1,16,256,256]{4,3,2,1,0:T(8,128)(2,1)S(1)}, bf16[1,1,16,256,256]{4,3,2,1,0:T(8,128)(2,1)}, u32[]{:S(2)}) %copy-start) | copy-done | bytes 2097176
  2.9 0.0 copy-start.1
  2.9 1.6 %copy-done.1 = bf16[1,1,16,256,256]{4,3,2,1,0:T(8,128)(2,1)S(1)} copy-done((bf16[1,1,16,256,256]{4,3,2,1,0:T(8,128)(2,1)S(1)}, bf16[1,1,16,256,256]{4,3,2,1,0:T(8,128)(2,1)}, u32[]{:S(2)}) %copy-start.1) | copy-done | bytes 2097176
  4.5 0.0 copy-start.2
  4.5 0.9 %copy-done.2 = bf16[1,1,256,256]{3,2,1,0:T(8,128)(2,1)S(1)} copy-done((bf16[1,1,256,256]{3,2,1,0:T(8,128)(2,1)S(1)}, bf16[1,1,256,256]{3,2,1,0:T(8,128)(2,1)}, u32[]{:S(2)}) %copy-start.2) | copy-done | bytes 131096
  5.4 0.0 copy-start.3
  5.4 0.7 %copy-done.3 = s32[1,1,16]{2,1,0:T(1,128)S(1)} copy-done((s32[1,1,16]{2,1,0:T(1,128)S(1)}, s32[1,1,16]{2,1,0:T(1,128)}, u32[]{:S(2)}) %copy-start.3) | copy-done | bytes 88
  6.0 41.9 %shard_map.68 = (bf16[256,256]{1,0:T(8,128)(2,1)S(1)}, bf16[256,256]{1,0:T(8,128)(2,1)S(1)}) custom-call(s32[16]{0:T(128)S(1)} %bitcast.13, s32[1]{0:T(128)} %bitcast.7.sizes, bf16[256,256]{1,0:T(8,128)(2,1)S(1)} %bitcast.12, bf16[16,256,256]{2,1,0:T(8,128)(2,1)S(1)} %bitcast.10, bf16[16,256,256]{2,1,0:T(8,128)(2,1)S(1)} %bitcast.11), custom_call_target="tpu_custom_call" | custom-call | flops 3221225472 | bytes 4194304 | tf_op jit(solution)/shard_map/pallas_call | solution.py:272
  47.9 0.7 %copy.10 = bf16[1,1,256,256]{3,2,1,0:T(8,128)(2,1)} copy(bf16[1,1,256,256]{3,2,1,0:T(8,128)(2,1)S(1)} %bitcast.9) | data formatting | bytes 262144
  48.6 0.7 %copy.11 = bf16[1,1,256,256]{3,2,1,0:T(8,128)(2,1)} copy(bf16[1,1,256,256]{3,2,1,0:T(8,128)(2,1)S(1)} %bitcast.8) | data formatting | bytes 262144
Async XLA Ops:
  1.3 1.6 %copy-start = (bf16[1,1,16,256,256]{4,3,2,1,0:T(8,128)(2,1)S(1)}, bf16[1,1,16,256,256]{4,3,2,1,0:T(8,128)(2,1)}, u32[]{:S(2)}) copy-start(bf16[1,1,16,256,256]{4,3,2,1,0:T(8,128)(2,1)} %param.6) | copy-start | bytes 6291460
  2.9 1.6 %copy-start.1 = (bf16[1,1,16,256,256]{4,3,2,1,0:T(8,128)(2,1)S(1)}, bf16[1,1,16,256,256]{4,3,2,1,0:T(8,128)(2,1)}, u32[]{:S(2)}) copy-start(bf16[1,1,16,256,256]{4,3,2,1,0:T(8,128)(2,1)} %param.7) | copy-start | bytes 6291460
  4.5 0.9 %copy-start.2 = (bf16[1,1,256,256]{3,2,1,0:T(8,128)(2,1)S(1)}, bf16[1,1,256,256]{3,2,1,0:T(8,128)(2,1)}, u32[]{:S(2)}) copy-start(bf16[1,1,256,256]{3,2,1,0:T(8,128)(2,1)} %param.5) | copy-start | bytes 393220
  5.4 0.7 %copy-start.3 = (s32[1,1,16]{2,1,0:T(1,128)S(1)}, s32[1,1,16]{2,1,0:T(1,128)}, u32[]{:S(2)}) copy-start(s32[1,1,16]{2,1,0:T(1,128)} %param.8) | copy-start | bytes 196

commit v2 on v1

--- a/solution.py
+++ b/solution.py
@@ -23,8 +23,8 @@
 
 
 def kernel(
-    nsec, nb, picks, sizes, wave_h, left_h, right_h, out1_h, out2_h,
-    wave_v, left, right, pool, fpool, inner, psend, precv, mine, rsend, rrecv, edge, inc, meta, acc,
+    nsec, nb, picks_h, sizes_h, wave_h, left_h, right_h, out1_h, out2_h,
+    picks, sizes, wave_v, left, right, pool, fpool, inner, psend, precv, mine, rsend, rrecv, edge, inc, meta, acc,
     stage, lsem, ssem, rsem,
 ):
     width = wave_h.shape[-1]
@@ -40,7 +40,11 @@
     load_wave = pltpu.make_async_copy(wave_h, wave_v, lsem.at[0])
     load_left = pltpu.make_async_copy(left_h, left, lsem.at[1])
     load_right = pltpu.make_async_copy(right_h, right, lsem.at[2])
+    load_sizes = pltpu.make_async_copy(sizes_h, sizes, lsem.at[5])
+    load_picks = pltpu.make_async_copy(picks_h, picks, lsem.at[6])
     load_wave.start()
+    load_sizes.start()
+    load_picks.start()
     load_left.start()
     load_right.start()
 
@@ -92,7 +96,9 @@
         for o in range(nx):
             arrived((name, "c", o), ref.at[((chip + nx - o) % nx) * 2 + 1 - core])
 
-    size = sizes[0]
+    load_sizes.wait()
+    load_picks.wait()
+    size = sizes[0, 0]
     live_at = (lax.broadcasted_iota(jnp.int32, (width, width), 0) < size) & (
         lax.broadcasted_iota(jnp.int32, (width, width), 1) < size
     )
@@ -108,7 +114,7 @@
     take("live", pool)
 
     for t in range(channels):
-        inner[:, t * width:(t + 1) * width] = dot(left[t], pool[picks[t]]).astype(BF16)
+        inner[:, t * width:(t + 1) * width] = dot(left[t], pool[picks[0, t]]).astype(BF16)
     total = dot(inner[...], right[...].reshape(channels * width, width))
     first = jnp.where(live_at, total, 0.0).astype(BF16)
     fpool[me] = first
@@ -220,7 +226,7 @@
         for d in range(nb):
             t = d * per + j
             left_two = (left[t].astype(F32) + inc[t].astype(F32)).astype(BF16)
-            step = dot(dot(left_two, fpool[picks[t]]).astype(BF16), right[t])
+            step = dot(dot(left_two, fpool[picks[0, t]]).astype(BF16), right[t])
             result = step if result is None else result + step
         acc[...] = result
 
@@ -266,15 +272,16 @@
     block = (width, width)
     copies = copies_between(nb, per)
     vmem = lambda *lead: pltpu.VMEM((*lead, *block), BF16)
-    anywhere = pl.BlockSpec(memory_space=pl.ANY)
-    smem = pl.BlockSpec(memory_space=pltpu.SMEM)
+    anywhere = pl.BlockSpec(memory_space=pltpu.HBM)
     out = jax.ShapeDtypeStruct(block, BF16)
     first, second = pl.pallas_call(
         functools.partial(kernel, nsec, nb),
         out_shape=(out, out),
-        in_specs=[smem, smem, anywhere, anywhere, anywhere],
+        in_specs=[anywhere] * 5,
         out_specs=(anywhere, anywhere),
         scratch_shapes=[
+            pltpu.SMEM((1, channels), jnp.int32),
+            pltpu.SMEM((1, 1), jnp.int32),
             vmem(),
             vmem(channels),
             vmem(channels),
@@ -291,19 +298,19 @@
             pltpu.VMEM((nb, 16, 128), F32),
             pltpu.VMEM(block, F32),
             vmem(),
-            pltpu.SemaphoreType.DMA((5,)),
+            pltpu.SemaphoreType.DMA((7,)),
             pltpu.SemaphoreType.DMA((copies,)),
             pltpu.SemaphoreType.DMA((copies,)),
         ],
         compiler_params=pltpu.CompilerParams(
-            collective_id=0, has_side_effects=True, vmem_limit_bytes=48 * 2**20
+            collective_id=0, has_side_effects=True, vmem_limit_bytes=62 * 2**20
         ),
         cost_estimate=pl.CostEstimate(
             flops=12 * channels * width**3, bytes_accessed=4 * channels * width**2, transcendentals=0
         ),
     )(
-        picks.reshape(channels),
-        sizes.reshape(1),
+        picks.reshape(1, channels),
+        sizes.reshape(1, 1),
         wave.reshape(block),
         left.reshape(channels, *block),
         right.reshape(channels, *block),

time: 49.5 us -> 46 us (0.929)
  local copies, waits for them, and re-layouts: 6.05 us -> 3.14 us
  Pallas kernels: 41.9 us -> 41.3 us
    unnamed x10 -> x2, local copies, waits for them, and re-layouts: 6.05 us -> 3.14 us
    pallas_call x1, Pallas kernels: 41.9 us -> 41.3 us  [shards(): pl.pallas_call(functools.partial(kernel, nsec, nb), out_shape=(out, out),...]
where the time goes in v2:
time: 46 us; the launch traced here: 45.8 us
  Pallas kernels  41.3 us (90%)
  local copies, waits for them, and re-layouts  3.14 us (7%)
  between operations  1.29 us (3%)
    pallas_call x1, Pallas kernels, shards(): pl.pallas_call(functools.partial(kernel, nsec, nb), out_shape=(out, out),...  41.3 us
    unnamed x2, local copies, waits for them, and re-layouts  3.14 us

profile of v2, /device:TPU:11, one launch (start us, length us, event | category | flops | bytes accessed | tf_op | source)
XLA Modules:
  0.0 45.8 jit_solution(13640055821992779647)
XLA Ops:
  1.3 41.3 %shard_map.68 = (bf16[256,256]{1,0:T(8,128)(2,1)}, bf16[256,256]{1,0:T(8,128)(2,1)}) custom-call(s32[1,16]{1,0:T(1,128)} %bitcast.11, s32[1,1]{1,0:T(1,128)S(6)} %copy.9.sizes_h, bf16[256,256]{1,0:T(8,128)(2,1)} %bitcast.10, bf16[16,256,256]{2,1,0:T(8,128)(2,1)} %bitcast.8, bf16[16,256,256]{2,1,0:T(8,128)(2,1)} %bitcast.9), custom_call_target="tpu_custom_call" | custom-call | flops 3221225472 | bytes 4194304 | tf_op jit(solution)/shard_map/pallas_call | solution.py:277
  42.6 1.6 %copy.10 = bf16[1,1,256,256]{3,2,1,0:T(8,128)(2,1)} copy(bf16[1,1,256,256]{3,2,1,0:T(8,128)(2,1)} %bitcast.7) | data formatting | bytes 262144
  44.2 1.6 %copy.11 = bf16[1,1,256,256]{3,2,1,0:T(8,128)(2,1)} copy(bf16[1,1,256,256]{3,2,1,0:T(8,128)(2,1)} %bitcast.6) | data formatting | bytes 262144

commit v3 on v2

--- a/solution.py
+++ b/solution.py
@@ -23,9 +23,9 @@
 
 
 def kernel(
-    nsec, nb, picks_h, sizes_h, wave_h, left_h, right_h, out1_h, out2_h,
+    nsec, nb, picks_h, sizes_h, wave_h, left_h, right_h, out1, out2,
     picks, sizes, wave_v, left, right, pool, fpool, inner, psend, precv, mine, rsend, rrecv, edge, inc, meta, acc,
-    stage, lsem, ssem, rsem,
+    lsem, ssem, rsem,
 ):
     width = wave_h.shape[-1]
     channels = left_h.shape[0]
@@ -40,8 +40,8 @@
     load_wave = pltpu.make_async_copy(wave_h, wave_v, lsem.at[0])
     load_left = pltpu.make_async_copy(left_h, left, lsem.at[1])
     load_right = pltpu.make_async_copy(right_h, right, lsem.at[2])
-    load_sizes = pltpu.make_async_copy(sizes_h, sizes, lsem.at[5])
-    load_picks = pltpu.make_async_copy(picks_h, picks, lsem.at[6])
+    load_sizes = pltpu.make_async_copy(sizes_h, sizes, lsem.at[3])
+    load_picks = pltpu.make_async_copy(picks_h, picks, lsem.at[4])
     load_wave.start()
     load_sizes.start()
     load_picks.start()
@@ -119,8 +119,7 @@
     first = jnp.where(live_at, total, 0.0).astype(BF16)
     fpool[me] = first
     share("first", fpool)
-    store_first = pltpu.make_async_copy(fpool.at[me], out1_h, lsem.at[3])
-    store_first.start()
+    out1[...] = first
 
     first_f = fpool[me].astype(F32)
     first_t = jnp.transpose(first_f).astype(BF16)
@@ -169,7 +168,6 @@
     count = jnp.sum(totals[8:], keepdims=True) * (1.0 / 1024)
     scale = lax.rsqrt(square_sum / count + 1e-06)
     factor = scale * scale * (1.0 / (width * math.sqrt(nb)))
-    store_first.wait()
     take("first", fpool)
 
     later = []
@@ -244,9 +242,7 @@
         if 3 <= tick < per + 3:
             second(tick - 3)
 
-    stage[...] = jnp.where(live_at, acc[...] * scale, 0.0).astype(BF16)
-    store_second = pltpu.make_async_copy(stage, out2_h, lsem.at[4])
-    store_second.start()
+    out2[...] = jnp.where(live_at, acc[...] * scale, 0.0).astype(BF16)
 
     for copy in sent:
         copy.wait_send()
@@ -261,7 +257,16 @@
         for copy in inner_sends:
             copy.wait_send()
 
-    store_second.wait()
+
+def write_out(first, second, first_h, second_h, sem):
+    copies = [
+        pltpu.make_async_copy(first, first_h, sem.at[0]),
+        pltpu.make_async_copy(second, second_h, sem.at[1]),
+    ]
+    for copy in copies:
+        copy.start()
+    for copy in copies:
+        copy.wait()
 
 
 def shards(nsec, nb, wave, left, right, picks, sizes):
@@ -273,12 +278,12 @@
     copies = copies_between(nb, per)
     vmem = lambda *lead: pltpu.VMEM((*lead, *block), BF16)
     anywhere = pl.BlockSpec(memory_space=pltpu.HBM)
-    out = jax.ShapeDtypeStruct(block, BF16)
+    out = pltpu.VMEM(block, BF16)
     first, second = pl.pallas_call(
         functools.partial(kernel, nsec, nb),
         out_shape=(out, out),
         in_specs=[anywhere] * 5,
-        out_specs=(anywhere, anywhere),
+        out_specs=(pl.BlockSpec(memory_space=pltpu.VMEM),) * 2,
         scratch_shapes=[
             pltpu.SMEM((1, channels), jnp.int32),
             pltpu.SMEM((1, 1), jnp.int32),
@@ -297,8 +302,7 @@
             vmem(channels),
             pltpu.VMEM((nb, 16, 128), F32),
             pltpu.VMEM(block, F32),
-            vmem(),
-            pltpu.SemaphoreType.DMA((7,)),
+            pltpu.SemaphoreType.DMA((5,)),
             pltpu.SemaphoreType.DMA((copies,)),
             pltpu.SemaphoreType.DMA((copies,)),
         ],
@@ -315,6 +319,15 @@
         left.reshape(channels, *block),
         right.reshape(channels, *block),
     )
+    result = jax.ShapeDtypeStruct(block, BF16)
+    first, second = pl.pallas_call(
+        write_out,
+        out_shape=(result, result),
+        in_specs=[pl.BlockSpec(memory_space=pltpu.VMEM)] * 2,
+        out_specs=(pl.BlockSpec(memory_space=pl.ANY),) * 2,
+        scratch_shapes=[pltpu.SemaphoreType.DMA((2,))],
+        compiler_params=pltpu.CompilerParams(has_side_effects=True),
+    )(*(pltpu.with_memory_space_constraint(x, pltpu.VMEM) for x in (first, second)))
     return first[None, None], second[None, None]
 
 

time: 46 us -> 43 us (0.935)
  local copies, waits for them, and re-layouts: 3.14 us -> 0 us
    unnamed x2 -> x0, local copies, waits for them, and re-layouts: 3.14 us -> none
    pallas_call x0 -> x1, Pallas kernels: none -> 0.72 us  [shards(): pl.pallas_call(write_out, out_shape=(result, result), in_specs=[pl.BlockS...]
    pallas_call x1, Pallas kernels: 41.3 us -> 40.7 us  [shards(): pl.pallas_call(functools.partial(kernel, nsec, nb), out_shape=(out, out),...]
where the time goes in v3:
time: 43 us; the launch traced here: 42.7 us
  Pallas kernels  41.4 us (96%)
  between operations  1.29 us (3%)
    pallas_call x1, Pallas kernels, shards(): pl.pallas_call(functools.partial(kernel, nsec, nb), out_shape=(out, out),...  40.7 us

profile of v3, /device:TPU:11, one launch (start us, length us, event | category | flops | bytes accessed | tf_op | source)
XLA Modules:
  0.0 42.7 jit_solution(13250370646542235703)
XLA Ops:
  1.3 40.7 %shard_map.68 = (bf16[256,256]{1,0:T(8,128)(2,1)S(1)}, bf16[256,256]{1,0:T(8,128)(2,1)S(1)}) custom-call(s32[1,16]{1,0:T(1,128)} %bitcast.11, s32[1,1]{1,0:T(1,128)S(6)} %copy.7.sizes_h, bf16[256,256]{1,0:T(8,128)(2,1)} %bitcast.8, bf16[16,256,256]{2,1,0:T(8,128)(2,1)} %bitcast.6, bf16[16,256,256]{2,1,0:T(8,128)(2,1)} %bitcast.7), custom_call_target="tpu_custom_call" | custom-call | flops 3221225472 | bytes 4194304 | tf_op jit(solution)/shard_map/pallas_call | solution.py:282
  42.0 0.7 %shard_map.69 = (bf16[256,256]{1,0:T(8,128)(2,1)}, bf16[256,256]{1,0:T(8,128)(2,1)}) custom-call(bf16[256,256]{1,0:T(8,128)(2,1)S(1)} %get-tuple-element.6.first, bf16[256,256]{1,0:T(8,128)(2,1)S(1)} %get-tuple-element.7.second), custom_call_target="tpu_custom_call" | custom-call | tf_op jit(solution)/shard_map/pallas_call | solution.py:323

commit v4 on v3

--- a/solution.py
+++ b/solution.py
@@ -19,18 +19,26 @@
 
 def copies_between(nb, per):
     nx = nb // 2
-    return 2 * (2 * nx - 1) + (nb - 1) + nx * per + (nx - 1) * per + per + per * (2 * nx - 1)
+    return (
+        2 * (2 * nx - 1) + (nb - 1) + nx * per + (nx - 1) * per + per + per * (2 * nx - 1)
+        + 2 * (nx - 1) * ahead(nb, per)
+    )
+
+
+def ahead(nb, per):
+    return 1 if per > 1 else 0
 
 
 def kernel(
     nsec, nb, picks_h, sizes_h, wave_h, left_h, right_h, out1, out2,
-    picks, sizes, wave_v, left, right, pool, fpool, inner, psend, precv, mine, rsend, rrecv, edge, inc, meta, acc,
+    picks, sizes, wave_v, left, right, pool, fpool, inner, psend, precv, mine, rsend, rrecv, edge, inc, meta, acc, lpre, tpre,
     lsem, ssem, rsem,
 ):
     width = wave_h.shape[-1]
     channels = left_h.shape[0]
     nx = nb // 2
     per = channels // nb
+    pre = ahead(nb, per)
     sec = lax.axis_index("sec")
     me = lax.axis_index("blk")
     chip = me // 2
@@ -109,8 +117,16 @@
     )
     share("live", pool)
     load_left.wait()
+    for o in range(1, nx):
+        for j in range(pre):
+            for c in range(2):
+                channel = (((chip + o) % nx) * 2 + c) * per + j
+                send(
+                    ("left", o, j, c), left.at[channel], lpre.at[((o - 1) * pre + j) * 2 + c],
+                    blk=same_core(o),
+                )
+    pass_on("live", pool)
     load_right.wait()
-    pass_on("live", pool)
     take("live", pool)
 
     for t in range(channels):
@@ -124,7 +140,17 @@
     first_f = fpool[me].astype(F32)
     first_t = jnp.transpose(first_f).astype(BF16)
 
-    rounds = [(o, j) for o in list(range(1, nx)) + [0] for j in range(per)]
+    rounds = [(o, j) for o in list(range(1, nx)) + [0] for j in range(pre, per)]
+    rounds += [(0, j) for j in range(pre)]
+
+    def partial(o, j, c):
+        channel = (((chip + o) % nx) * 2 + c) * per + j
+        term = dot(first_t, dot(left[channel], fpool[me]).astype(BF16))
+        if j < pre:
+            for p in range(1, nx):
+                lv = dot(lpre[((p - 1) * pre + j) * 2 + c], fpool[same_core(nx - p)]).astype(BF16)
+                term = term + dot(tpre[p - 1], lv)
+        return term.astype(BF16)
 
     def combine(r):
         o, j = rounds[r]
@@ -139,14 +165,17 @@
             send(("rs", o, j), rsend.at[slot], rrecv.at[slot], blk=same_core(o))
 
     for r, (o, j) in enumerate(rounds):
-        q = (chip + o) % nx
-        theirs = (q * 2 + 1 - core) * per + j
-        own = (q * 2 + core) * per + j
-        lv = dot(left[theirs], fpool[me]).astype(BF16)
-        psend[r] = dot(first_t, lv).astype(BF16)
+        if j < pre and j == 0:
+            pass_on("first", fpool)
+            for p in range(1, nx):
+                tpre[p - 1] = jnp.transpose(fpool[same_core(nx - p)].astype(F32)).astype(BF16)
+                for i in range(pre):
+                    for c in range(2):
+                        slot = ((p - 1) * pre + i) * 2 + c
+                        arrived(("left", p, i, c), lpre.at[slot])
+        psend[r] = partial(o, j, 1 - core)
         send(("part", r), psend.at[r], precv.at[r], blk=sib)
-        lv = dot(left[own], fpool[me]).astype(BF16)
-        mine[r] = dot(first_t, lv).astype(BF16)
+        mine[r] = partial(o, j, core)
         if r == 0:
             squares = jnp.sum((first_f * first_f).reshape(width // 8, 8, width), axis=0)
             fold = squares[:, :128]
@@ -160,7 +189,8 @@
             combine(r - 1)
     combine(len(rounds) - 1)
 
-    pass_on("first", fpool)
+    if not pre:
+        pass_on("first", fpool)
     for p in range(1, nb):
         arrived(("meta", p), meta.at[(me + nb - p) % nb])
     totals = jnp.sum(meta[...], axis=0)
@@ -174,7 +204,7 @@
 
     def up(j):
         result = edge[j].astype(F32)
-        for o in range(1, nx):
+        for o in range(1, nx if j >= pre else 1):
             slot = (o - 1) * per + j
             arrived(("rs", o, j), rrecv.at[slot])
             result = result + rrecv[slot].astype(F32)
@@ -276,6 +306,7 @@
     per = channels // nb
     block = (width, width)
     copies = copies_between(nb, per)
+    pre = ahead(nb, per)
     vmem = lambda *lead: pltpu.VMEM((*lead, *block), BF16)
     anywhere = pl.BlockSpec(memory_space=pltpu.HBM)
     out = pltpu.VMEM(block, BF16)
@@ -302,6 +333,8 @@
             vmem(channels),
             pltpu.VMEM((nb, 16, 128), F32),
             pltpu.VMEM(block, F32),
+            vmem(max(1, 2 * (nx - 1) * pre)),
+            vmem(nx - 1),
             pltpu.SemaphoreType.DMA((5,)),
             pltpu.SemaphoreType.DMA((copies,)),
             pltpu.SemaphoreType.DMA((copies,)),

time: 43 us -> 40.3 us (0.937)
  Pallas kernels: 41.4 us -> 38.8 us
    pallas_call x1, Pallas kernels: 40.7 us -> 38.1 us  [shards(): pl.pallas_call(functools.partial(kernel, nsec, nb), out_shape=(out, out),...]
where the time goes in v4:
time: 40.3 us; the launch traced here: 40.1 us
  Pallas kernels  38.8 us (96%)
  between operations  1.29 us (3%)
    pallas_call x1, Pallas kernels, shards(): pl.pallas_call(functools.partial(kernel, nsec, nb), out_shape=(out, out),...  38.1 us

profile of v4, /device:TPU:11, one launch (start us, length us, event | category | flops | bytes accessed | tf_op | source)
XLA Modules:
  0.0 40.1 jit_solution(14803045350849249265)
XLA Ops:
  1.3 38.1 %shard_map.68 = (bf16[256,256]{1,0:T(8,128)(2,1)S(1)}, bf16[256,256]{1,0:T(8,128)(2,1)S(1)}) custom-call(s32[1,16]{1,0:T(1,128)} %bitcast.11, s32[1,1]{1,0:T(1,128)S(6)} %copy.7.sizes_h, bf16[256,256]{1,0:T(8,128)(2,1)} %bitcast.8, bf16[16,256,256]{2,1,0:T(8,128)(2,1)} %bitcast.6, bf16[16,256,256]{2,1,0:T(8,128)(2,1)} %bitcast.7), custom_call_target="tpu_custom_call" | custom-call | flops 3221225472 | bytes 4194304 | tf_op jit(solution)/shard_map/pallas_call | solution.py:313
  39.4 0.7 %shard_map.69 = (bf16[256,256]{1,0:T(8,128)(2,1)}, bf16[256,256]{1,0:T(8,128)(2,1)}) custom-call(bf16[256,256]{1,0:T(8,128)(2,1)S(1)} %get-tuple-element.6.first, bf16[256,256]{1,0:T(8,128)(2,1)S(1)} %get-tuple-element.7.second), custom_call_target="tpu_custom_call" | custom-call | tf_op jit(solution)/shard_map/pallas_call | solution.py:356

commit v5 on v4

--- a/solution.py
+++ b/solution.py
@@ -245,17 +245,19 @@
                 copy.start()
 
     def second(j):
-        @pl.when(sec > 0)
-        def _():
+        result = acc[...] if j else None
+        for c in (core, 1 - core):
             for o in range(nx):
-                arrived(("inc", j, "c", o), inc.at[(((chip + nx - o) % nx) * 2 + 1 - core) * per + j])
-
-        result = acc[...] if j else None
-        for d in range(nb):
-            t = d * per + j
-            left_two = (left[t].astype(F32) + inc[t].astype(F32)).astype(BF16)
-            step = dot(dot(left_two, fpool[picks[0, t]]).astype(BF16), right[t])
-            result = step if result is None else result + step
+                t = (((chip + nx - o) % nx) * 2 + c) * per + j
+                if c is not core:
+
+                    @pl.when(sec > 0)
+                    def _():
+                        arrived(("inc", j, "c", o), inc.at[t])
+
+                left_two = (left[t].astype(F32) + inc[t].astype(F32)).astype(BF16)
+                step = dot(dot(left_two, fpool[picks[0, t]]).astype(BF16), right[t])
+                result = step if result is None else result + step
         acc[...] = result
 
     @pl.when(sec == 0)

time: 40.3 us -> 40.1 us (level)
  no operation moved by 1% of the time
where the time goes in v5:
time: 40.1 us; the launch traced here: 39.9 us
  Pallas kernels  38.6 us (96%)
  between operations  1.29 us (3%)
    pallas_call x1, Pallas kernels, shards(): pl.pallas_call(functools.partial(kernel, nsec, nb), out_shape=(out, out),...  37.9 us

profile of v5, /device:TPU:11, one launch (start us, length us, event | category | flops | bytes accessed | tf_op | source)
XLA Modules:
  0.0 39.9 jit_solution(4800929444129756389)
XLA Ops:
  1.3 37.9 %shard_map.68 = (bf16[256,256]{1,0:T(8,128)(2,1)S(1)}, bf16[256,256]{1,0:T(8,128)(2,1)S(1)}) custom-call(s32[1,16]{1,0:T(1,128)} %bitcast.11, s32[1,1]{1,0:T(1,128)S(6)} %copy.7.sizes_h, bf16[256,256]{1,0:T(8,128)(2,1)} %bitcast.8, bf16[16,256,256]{2,1,0:T(8,128)(2,1)} %bitcast.6, bf16[16,256,256]{2,1,0:T(8,128)(2,1)} %bitcast.7), custom_call_target="tpu_custom_call" | custom-call | flops 3221225472 | bytes 4194304 | tf_op jit(solution)/shard_map/pallas_call | solution.py:315
  39.2 0.7 %shard_map.69 = (bf16[256,256]{1,0:T(8,128)(2,1)}, bf16[256,256]{1,0:T(8,128)(2,1)}) custom-call(bf16[256,256]{1,0:T(8,128)(2,1)S(1)} %get-tuple-element.6.first, bf16[256,256]{1,0:T(8,128)(2,1)S(1)} %get-tuple-element.7.second), custom_call_target="tpu_custom_call" | custom-call | tf_op jit(solution)/shard_map/pallas_call | solution.py:358
